TPU v7x, 128 devices: a whole 4x4x4 slice. The times are simulated.
128 devices in a mesh: role: 4 (over x), grp: 32 (over z, y, core).
Axes of the slice: x: 4, y: 4, z: 4, core: 2. Of those that a mesh axis runs over, the one named last changes fastest.
Arguments:
- queries: bfloat16 [32, 16, 128, 576], P('grp', 'role'), may hold values from -400 to 400
- compressed_cache: bfloat16 [32, 16, 512, 576], P('grp', 'role'), may hold values from -7 to 7
- lengths: int32 [32, 16], P('grp', 'role'), may hold values from 16 to 512, as said below
- value_expand_matrix: bfloat16 [128, 512, 128], P(('role', 'grp')), may hold values from -0.25 to 0.25
- out_proj: bfloat16 [16384, 7168], P(('role', 'grp')), may hold values from -0.1875 to 0.1875
- residual: bfloat16 [32, 16, 7168], P('grp', 'role'), may hold values from -4 to 4
- norm_gain: bfloat16 [7168], replicated, may hold values from 0.25 to 1.75
- expert_ids: int32 [32, 16, 8], P('grp', 'role'), may hold values from 0 to 31, all different within a row; in each aligned block of 16 rows (0 to 15, 16 to 31, ..., all dimensions but the last counted through in order) at most 6 rows name the same one
- expert_gates: bfloat16 [32, 16, 8], P('grp', 'role'), may hold values from 0.099609375 to 0.59765625
- w_gate: bfloat16 [32, 7168, 2048], P('grp', None, 'role'), may hold values from -0.0625 to 0.0625
- w_up: bfloat16 [32, 7168, 2048], P('grp', None, 'role'), may hold values from -0.0625 to 0.0625
- w_down: bfloat16 [32, 2048, 7168], P('grp', 'role'), may hold values from -0.125 to 0.125
Outputs:
- layer_out: bfloat16 [32, 16, 7168], P('grp', 'role')
Inputs may be any that keep to these rules, and one draw needn't show every extreme that they name: `expert_ids`: each token names 8 different experts. In every aligned block of 16 tokens (the tokens of one index of grp) no expert is named by more than 6 tokens; in some blocks one is named by exactly 6. `lengths`: some request has all 512 slots live.
All inputs are finite; a program needn't handle non-finite values.
Results may differ from a plain program's by a relative error of at most 0.015.
Values may be sent and summed in bfloat16 or wider, within the bound.
A program may use at most 128 MiB of HBM per device.

v0:
```python
import jax
import jax.numpy as jnp
from jax import lax
from jax.sharding import PartitionSpec as P

TOPK = 8


score_scale = 192.0 ** (-0.5)
norm_eps = 1e-06


def run_expert(in_rows, weight_gate, weight_up, weight_down):
    flat_rows = in_rows.reshape(-1, in_rows.shape[-1])
    gate_proj = jnp.dot(flat_rows, weight_gate, preferred_element_type=jnp.float32)
    up_proj = jnp.dot(flat_rows, weight_up, preferred_element_type=jnp.float32)
    activated = (jax.nn.silu(gate_proj) * up_proj).astype(jnp.bfloat16)
    down_proj = jnp.dot(activated, weight_down, preferred_element_type=jnp.float32)
    return down_proj.reshape(in_rows.shape[:-1] + (weight_down.shape[1],))


def per_device(
    queries,
    compressed_cache,
    lengths,
    value_expand_matrix,
    out_proj,
    residual,
    norm_gain,
    expert_ids,
    expert_gates,
    w_gate,
    w_up,
    w_down,
):
    query_rows = queries[0]
    cache_rows = compressed_cache[0]
    length_rows = lengths[0]
    latent_width = value_expand_matrix.shape[1]
    context = cache_rows.shape[1]
    tok_here = query_rows.shape[0]
    scores = (
        jnp.einsum("thk,tck->thc", query_rows, cache_rows, preferred_element_type=jnp.float32)
        * score_scale
    )
    live_keys = jnp.arange(context, dtype=jnp.int32)[None, None, :] < length_rows[:, None, None]
    row_max = jnp.max(jnp.where(live_keys, scores, -1e30), axis=-1, keepdims=True)
    exp_terms = jnp.exp(jnp.where(live_keys, scores - row_max, -1e30))
    exp_total = jnp.sum(exp_terms, axis=-1, keepdims=True)
    weighted_sum = (
        jnp.einsum(
            "thc,tck->thk",
            exp_terms.astype(jnp.bfloat16),
            cache_rows[:, :, :latent_width],
            preferred_element_type=jnp.float32,
        )
        / exp_total
    )
    latent_result = weighted_sum.astype(jnp.bfloat16)
    per_head_split = lax.all_to_all(
        latent_result, ("role", "grp"), split_axis=1, concat_axis=0, tiled=True
    )
    value_rows = jnp.einsum(
        "gri,rix->grx", per_head_split, value_expand_matrix, preferred_element_type=jnp.float32
    ).astype(jnp.bfloat16)
    attention = lax.psum_scatter(
        jnp.dot(
            value_rows.reshape(tok_here * lax.axis_size(("role", "grp")), -1),
            out_proj,
            preferred_element_type=jnp.float32,
        ),
        ("role", "grp"),
        scatter_dimension=0,
        tiled=True,
    )
    stream = residual[0].astype(jnp.float32) + attention
    scale_rows = lax.rsqrt(jnp.mean(stream * stream, axis=-1, keepdims=True) + norm_eps)
    normed = (stream * scale_rows * norm_gain.astype(jnp.float32)).astype(jnp.bfloat16)
    role_count = lax.axis_size("role")
    group_count = lax.axis_size("grp")
    expert_count = group_count * w_gate.shape[0]
    weight_gate = w_gate[0]
    weight_up = w_up[0]
    weight_down = w_down[0]
    route_ids = expert_ids[0]
    gate_values = expert_gates[0].astype(jnp.float32)
    picked = route_ids[:, :, None] == jnp.arange(expert_count, dtype=jnp.int32)[None, None, :]
    gate_table = jnp.sum(jnp.where(picked, gate_values[:, :, None], 0.0), axis=1)
    group_rows, group_table = (
        lax.all_gather(normed[None], "role", axis=1, tiled=True),
        lax.all_gather(gate_table.astype(jnp.bfloat16)[None], "role", axis=1, tiled=True),
    )
    grp_tok = tok_here * role_count
    slot_count = min(grp_tok, (3 * grp_tok * TOPK + 2 * expert_count - 1) // (2 * expert_count))
    route_hit = (group_table[0] != 0).astype(jnp.int32)
    before = jnp.cumsum(route_hit, axis=0) - route_hit
    slots = jnp.arange(slot_count, dtype=jnp.int32)
    slot_place = (route_hit[:, :, None] == 1) & (before[:, :, None] == slots[None, None, :])
    slot_onehot = slot_place.astype(jnp.bfloat16)
    send_rows = jnp.einsum(
        "tec,td->ecd", slot_onehot, group_rows[0], preferred_element_type=jnp.float32
    ).astype(jnp.bfloat16)
    partial_value = run_expert(
        lax.all_to_all(send_rows, "grp", split_axis=0, concat_axis=0, tiled=True),
        weight_gate,
        weight_up,
        weight_down,
    )
    weighted = slot_place.astype(jnp.float32) * group_table[0].astype(jnp.float32)[:, :, None]
    full_sum = lax.psum(partial_value.astype(jnp.bfloat16), "role").astype(jnp.float32)
    back_rows = lax.all_to_all(
        full_sum.astype(jnp.bfloat16), "grp", split_axis=0, concat_axis=0, tiled=True
    ).astype(full_sum.dtype)
    own_weights = lax.dynamic_slice_in_dim(weighted, lax.axis_index("role") * tok_here, tok_here, 0)
    expert_sum = jnp.einsum("tec,ecd->td", own_weights, back_rows, precision=lax.Precision.HIGHEST)
    return (stream + expert_sum).astype(jnp.bfloat16)[None]


def solution(mesh):
    in_specs = (
        P("grp", "role", None, None),
        P("grp", "role", None, None),
        P("grp", "role"),
        P(("role", "grp"), None, None),
        P(("role", "grp"), None),
        P("grp", "role", None),
        P(),
        P("grp", "role", None),
        P("grp", "role", None),
        P("grp", None, "role"),
        P("grp", None, "role"),
        P("grp", "role", None),
    )
    out_specs = P("grp", "role", None)
    return jax.shard_map(
        per_device, mesh=mesh, in_specs=in_specs, out_specs=out_specs, check_vma=False
    )
```

profile of v0, /device:TPU:0, one launch (start us, length us, event | category | flops | bytes accessed | tf_op | source)
XLA Modules:
  0.0 442.2 jit_solution(17413118075015713675)
XLA Ops:
  6.5 4.5 %copy.26 = bf16[1,4,512,576]{3,2,1,0:T(8,128)(2,1)} copy(bf16[1,4,512,576]{2,3,1,0:T(8,128)(2,1)} %param.13) | data formatting | bytes 4718592 | tf_op args[1]
  11.0 2.4 fusion.14
  13.5 0.1 iota_compare_fusion.2
  13.6 0.4 fusion.55
  14.0 0.4 fusion.28
  14.4 0.4 copy.28
  14.8 24.5 %all_to_all.25 = bf16[4,128,512]{2,0,1:T(4,128)(2,1)S(1)} all-to-all(bf16[4,128,512]{2,0,1:T(4,128)(2,1)S(1)} %copy.28), channel_id=1, replica_groups=mesh['role'=4,'grp'=32] {'role','grp'}, dimensions={1} | all-to-all | bytes 1048576 | tf_op jit(solution)/shard_map/all_to_all | solution.py:60
  39.3 0.1 reshape.102
  39.5 6.5 %fusion.37 = f32[512,7168]{1,0:T(8,128)} fusion(bf16[128,7168]{1,0:T(8,128)(2,1)S(1)} %copy-done, bf16[512,512]{1,0:T(8,128)(2,1)S(1)} %reshape.102, bf16[1,512,128]{2,1,0:T(8,128)(2,1)S(1)} %copy-done.6), kind=kOutput, calls=%fused_computation.28 | convolution fusion | flops 1006698496 | bytes 17170432 | tf_op jit(solution)/shard_map/dot_general | solution.py:67
  46.0 0.0 all-reduce.6.cloned.1.call-update
  46.0 0.0 all-reduce.4.cloned.1.call-start
  46.0 0.6 copy-done.7
  46.7 0.1 select_reduce_fusion.1
  46.8 8.1 %all-gather.2 = bf16[4,4,32]{2,1,0:T(4,128)(2,1)S(1)} all-gather(bf16[1,4,32]{2,1,0:T(4,128)(2,1)S(1)} %bitcast.76), channel_id=2, replica_groups=mesh['role'=4,'grp'=32] {'role'}, dimensions={0}, use_global_device_ids=true | all-gather | bytes 1280 | tf_op jit(solution)/shard_map/all_gather | solution.py:91
  55.0 160.7 %all-reduce.6.cloned.1.call-done = f32[512,7168]{1,0:T(8,128)} async-done(((f32[512,7168]{1,0:T(8,128)}), f32[512,7168]{1,0:T(8,128)}) %all-reduce.6.cloned.1.call-update) | async-done | bytes 14680080
  215.7 1.1 multiply_reduce_fusion
  216.8 1.0 fusion.45
  217.8 12.2 %all-gather.3 = bf16[4,4,7168]{2,1,0:T(4,128)(2,1)S(1)} all-gather(bf16[1,4,7168]{2,1,0:T(4,128)(2,1)S(1)} %fusion.45), channel_id=3, replica_groups=mesh['role'=4,'grp'=32] {'role'}, dimensions={0}, use_global_device_ids=true | all-gather | bytes 286720 | tf_op jit(solution)/shard_map/all_gather | solution.py:90
  230.0 0.1 reshape.126
  230.1 0.9 convolution_convert_fusion.1
  231.0 1.5 copy.29
  232.5 50.6 %all_to_all.26 = bf16[32,6,7168]{2,1,0:T(8,128)(2,1)} all-to-all(bf16[32,6,7168]{2,1,0:T(8,128)(2,1)S(1)} %copy.29), channel_id=1, replica_groups=mesh['role'=4,'grp'=32] {'grp'}, dimensions={0} | all-to-all | bytes 5505024 | tf_op jit(solution)/shard_map/all_to_all | solution.py:104
  283.1 4.6 %reshape.104 = bf16[192,7168]{1,0:T(8,128)(2,1)} reshape(bf16[32,6,7168]{2,1,0:T(8,128)(2,1)} %all_to_all.26) | data formatting | bytes 5505024 | tf_op jit(solution)/shard_map/reshape | solution.py:14
  287.8 5.6 %fusion.7 = f32[192,512]{1,0:T(8,128)S(1)} fusion(bf16[192,7168]{1,0:T(8,128)(2,1)} %reshape.104, bf16[1,7168,512]{2,1,0:T(8,128)(2,1)} %param.21), kind=kOutput, calls=%fused_computation.10 | convolution fusion | flops 1409286144 | bytes 10485760 | tf_op jit(solution)/shard_map/dot_general | solution.py:15
  293.4 4.7 %fusion.34 = bf16[192,512]{1,0:T(8,128)(2,1)S(1)} fusion(bf16[192,7168]{1,0:T(8,128)(2,1)S(1)} %copy-done.2, bf16[1,7168,512]{2,1,0:T(8,128)(2,1)} %param.22, f32[192,512]{1,0:T(8,128)S(1)} %fusion.7), kind=kOutput, calls=%fused_computation.26 | convolution fusion | flops 1409875968 | bytes 10682368 | tf_op jit(solution)/shard_map/dot_general | solution.py:16
  298.2 0.1 dot_general.36
  298.3 6.2 %convolution_convert_fusion = bf16[32,6,7168]{2,0,1:T(8,128)(2,1)} fusion(bf16[1,512,7168]{2,1,0:T(8,128)(2,1)} %param.23, bf16[32,6,512]{2,1,0:T(8,128)(2,1)S(1)} %dot_general.36), kind=kOutput, calls=%fused_computation.1 | convolution fusion | flops 1410662400 | bytes 10289152 | tf_op jit(solution)/shard_map/dot_general | solution.py:18
  304.5 65.5 %all-reduce.4.cloned.1.call-done = bf16[32,6,7168]{2,0,1:T(8,128)(2,1)} async-done(((bf16[32,6,7168]{2,0,1:T(8,128)(2,1)}), bf16[32,6,7168]{2,0,1:T(8,128)(2,1)}) %all-reduce.4.cloned.1.call-update) | async-done | bytes 2752528 | tf_op jit(solution)/shard_map/psum | solution.py:110
  370.0 5.2 %copy.31 = bf16[32,6,7168]{2,1,0:T(8,128)(2,1)} copy(bf16[32,6,7168]{2,0,1:T(8,128)(2,1)} %all-reduce.4.cloned.1.call-done) | data formatting | bytes 5505024 | tf_op jit(solution)/shard_map/psum | solution.py:110
  375.2 7.4 %all-to-all-start.2 = ((bf16[32,6,7168]{2,1,0:T(8,128)(2,1)}), bf16[32,6,7168]{2,1,0:T(8,128)(2,1)}, u32[]{:S(2)}, u32[]{:S(2)}) async-start(bf16[32,6,7168]{2,1,0:T(8,128)(2,1)} %copy.31), calls=%async_computation.2 | async-start | bytes 7340032 | tf_op jit(solution)/shard_map/all_to_all | solution.py:111
  382.6 47.6 %all-to-all-done.2 = bf16[32,6,7168]{2,1,0:T(8,128)(2,1)} async-done(((bf16[32,6,7168]{2,1,0:T(8,128)(2,1)}), bf16[32,6,7168]{2,1,0:T(8,128)(2,1)}, u32[]{:S(2)}, u32[]{:S(2)}) %all-to-all-start.2) | async-done | bytes 2752544 | tf_op jit(solution)/shard_map/all_to_all | solution.py:111
  430.2 5.1 %fusion.3 = bf16[1,4,7168]{2,1,0:T(4,128)(2,1)} fusion(bf16[32,6,7168]{2,1,0:T(8,128)(2,1)} %all-to-all-done.2, pred[16,32,6]{1,0,2:T(8,128)(4,1)S(1)} %fusion.46, s32[]{:T(128)S(6)} %select_n.17, f32[4,32]{1,0:T(4,128)S(1)} %constant_dynamic-slice_fusion, f32[512,7168]{1,0:T(8,128)} %all-reduce.6.cloned.1.call-done, u32[]{:T(128)S(6)} %multiply.7, ...), kind=kOutput, calls=%fused_computation.6 | convolution fusion | flops 66175744 | bytes 2987016 | tf_op jit(solution)/shard_map/tec,ecd->td/dot_general | solution.py:115
  (33 shorter events, 0.2 us)
Async XLA Ops:
  6.5 32.9 %copy-start = (bf16[128,7168]{1,0:T(8,128)(2,1)S(1)}, bf16[128,7168]{1,0:T(8,128)(2,1)}, u32[]{:S(2)}) copy-start(bf16[128,7168]{1,0:T(8,128)(2,1)} %param.16) | copy-start | bytes 5505028
  6.5 4.5 %copy-start.4 = (bf16[1,4,128,576]{2,3,1,0:T(8,128)(2,1)S(1)}, bf16[1,4,128,576]{2,3,1,0:T(8,128)(2,1)}, u32[]{:S(2)}) copy-start(bf16[1,4,128,576]{2,3,1,0:T(8,128)(2,1)} %param.12) | copy-start | bytes 1769476
  6.5 209.1 %all-reduce.6.cloned.1.call-start = ((), (), s32[]{:S(2)}) async-start(), calls=%async_computation.4 | async-start | bytes 29360128
  11.0 2.5 copy-start.10
  11.0 2.9 copy-start.3
  14.4 25.1 %copy-start.6 = (bf16[1,512,128]{2,1,0:T(8,128)(2,1)S(1)}, bf16[1,512,128]{2,1,0:T(8,128)(2,1)}, u32[]{:S(2)}) copy-start(bf16[1,512,128]{2,1,0:T(8,128)(2,1)} %param.15) | copy-start | bytes 393220
  46.0 0.7 copy-start.7
  46.0 0.7 copy-start.9
  46.0 0.7 copy-start.8
  46.0 169.7 %copy-start.5 = (bf16[1,4,7168]{2,1,0:T(4,128)(2,1)S(1)}, bf16[1,4,7168]{2,1,0:T(4,128)(2,1)}, u32[]{:S(2)}) copy-start(bf16[1,4,7168]{2,1,0:T(4,128)(2,1)} %param.17) | copy-start | bytes 172036
  46.0 324.0 %all-reduce.4.cloned.1.call-start = ((), (), s32[]{:S(2)}) async-start(), calls=%async_computation.3 | async-start | bytes 5505024 | tf_op jit(solution)/shard_map/psum | solution.py:110
  287.8 5.6 %copy-start.2 = (bf16[192,7168]{1,0:T(8,128)(2,1)S(1)}, bf16[192,7168]{1,0:T(8,128)(2,1)}, u32[]{:S(2)}) copy-start(bf16[192,7168]{1,0:T(8,128)(2,1)} %reshape.104) | copy-start | bytes 8257540
  375.2 55.1 %all-to-all-start.2 = ((bf16[32,6,7168]{2,1,0:T(8,128)(2,1)}), bf16[32,6,7168]{2,1,0:T(8,128)(2,1)}, u32[]{:S(2)}, u32[]{:S(2)}) async-start(bf16[32,6,7168]{2,1,0:T(8,128)(2,1)} %copy.31), calls=%async_computation.2 | async-start | bytes 7340032 | tf_op jit(solution)/shard_map/all_to_all | solution.py:111
  382.6 52.8 %copy-start.1 = (bf16[128,7168]{1,0:T(8,128)(2,1)S(1)}, bf16[128,7168]{1,0:T(8,128)(2,1)}, u32[]{:S(2)}) copy-start(bf16[128,7168]{1,0:T(8,128)(2,1)} %param.16) | copy-start | bytes 5505028
Sparse Core Ops, SparseCore 0:
  46.1 169.5 all-reduce.5
  304.6 65.3 all-reduce.3
where the time goes:
time: 443 us; the launch traced here: 442 us
  waiting for transfers between devices  274 us (62%)
  blocking collectives  95.4 us (22%)
  matrix products  31.9 us (7%)
  local copies, waits for them, and re-layouts  17.2 us (4%)
  between operations  13.6 us (3%)
  starting transfers between devices  7.42 us (2%)
    unnamed x3, waiting for transfers between devices  161 us
    psum x1, waiting for transfers between devices, per_device(): lax.psum(partial_value.astype(jnp.bfloat16), 'role').astype(jnp.float32)  65.5 us
    all_to_all x1, blocking collectives, per_device(): lax.all_to_all(send_rows, 'grp', split_axis=0, concat_axis=0, tiled=True)  50.6 us
    all_to_all x1, waiting for transfers between devices, per_device(): lax.all_to_all(full_sum.astype(jnp.bfloat16), 'grp', split_axis=0, concat...  47.6 us
    all_to_all x1, blocking collectives, per_device(): lax.all_to_all(latent_result, ('role', 'grp'), split_axis=1, concat_axis=...  24.5 us
    all_gather x1, blocking collectives, per_device(): lax.all_gather(normed[None], 'role', axis=1, tiled=True)  12.2 us
  transfers between devices with their start and end apart: 3, of which 3 were waited for; matrix products, arithmetic and copies ran while one was open for 0% of the time, Pallas kernels for 0%

commit v1 on v0

v1 whole, which is shorter than its diff:
```python
import jax
import jax.numpy as jnp
from jax import lax
from jax.experimental import pallas as pl
from jax.experimental.pallas import tpu as pltpu
from jax.sharding import PartitionSpec as P

MESH = pl.DeviceIdType.MESH
F32 = jnp.float32
BF16 = jnp.bfloat16

score_scale = 192.0 ** (-0.5)
norm_eps = 1e-06

D = 7168
QUARTER = 1792
PARTS = (
    (0, 640, (0, 1, 2)),
    (640, 640, (1, 2, 0)),
    (1280, 512, (2, 0, 1)),
)
WIDE = 640


def coordinates():
    grp = lax.axis_index("grp")
    return lax.axis_index("role"), grp // 8, (grp // 2) % 4, grp % 2


def device(x, z, y, c):
    return {"role": x, "grp": z * 8 + y * 2 + c}


def dot(a, b):
    return jnp.dot(a, b, preferred_element_type=F32)


def onehot(shape, source_of_row):
    rows = lax.broadcasted_iota(jnp.int32, shape, 0)
    columns = lax.broadcasted_iota(jnp.int32, shape, 1)
    return (columns == source_of_row(rows)).astype(BF16)


def kernel(
    len_ref,
    res_ref,
    gain_ref,
    ids_ref,
    gates_ref,
    q_hbm,
    cache_hbm,
    ve_hbm,
    op_hbm,
    wg_hbm,
    wu_hbm,
    wd_hbm,
    out_ref,
    q_buf,
    cache_buf,
    op_buf,
    wg_buf,
    wu_buf,
    wd_buf,
    ve_buf,
    a2a_send,
    a2a_recv,
    val_f32,
    val_send,
    val_recv,
    p_a,
    p_b,
    p_c,
    r1_a,
    r1_b,
    r1_c,
    s1_a,
    s1_b,
    s1_c,
    r2_a,
    r2_b,
    r2_c,
    s2_a,
    s2_b,
    s2_c,
    r3_a,
    r3_b,
    r3_c,
    n_a,
    n_b,
    n_c,
    stream_buf,
    acc_g,
    acc_u,
    act_buf,
    far_a,
    far_b,
    far_c,
    last_send,
    load_sem,
    ve_send_sem,
    ve_recv_sem,
    op_send_sem,
    op_recv_sem,
    a2a_send_sem,
    a2a_recv_sem,
    val_send_sem,
    val_recv_sem,
    rs_send_sem,
    rs_recv_sem,
    ag_send_sem,
    ag_recv_sem,
    pair_send_sem,
    pair_recv_sem,
    far_send_sem,
    far_recv_sem,
    last_send_sem,
    last_recv_sem,
):
    x, z, y, c = coordinates()
    zy = z * 4 + y
    other = 1 - c
    here = (x, z, y)
    me = device(x, z, y, c)
    sibling = device(x, z, y, other)
    sends = []

    def peer(axis, step):
        at = [x, z, y]
        at[axis] = (at[axis] + step) % 4
        return device(at[0], at[1], at[2], c)

    def remote(src, dst, send_sem, recv_sem, to):
        return pltpu.make_async_remote_copy(
            src_ref=src,
            dst_ref=dst,
            send_sem=send_sem,
            recv_sem=recv_sem,
            device_id=to,
            device_id_type=MESH,
        )

    def send(src, dst, send_sem, recv_sem, to):
        copy = remote(src, dst, send_sem, recv_sem, to)
        copy.start()
        sends.append(copy)

    def arrived(dst, send_sem, recv_sem):
        remote(dst, dst, send_sem, recv_sem, me).wait_recv()

    def zy_peer(step):
        p = (zy + step) % 16
        return p, device(x, p // 4, p % 4, c)

    barrier = pltpu.get_barrier_semaphore()

    def greet(step, carry):
        _, to = zy_peer(step)
        pl.semaphore_signal(barrier, inc=1, device_id=to, device_id_type=MESH)
        return carry

    lax.fori_loop(1, 16, greet, 0)
    for step in range(1, 4):
        for core in (c, other):
            pl.semaphore_signal(
                barrier, inc=1, device_id=device((x + step) % 4, z, y, core), device_id_type=MESH
            )
    pl.semaphore_signal(barrier, inc=1, device_id=sibling, device_id_type=MESH)

    load_q = pltpu.make_async_copy(q_hbm.at[0], q_buf, load_sem.at[0])
    load_cache = pltpu.make_async_copy(cache_hbm.at[0], cache_buf, load_sem.at[1])
    ve_own = ve_buf.at[x, :, pl.ds(pl.multiple_of(c * 128, 128), 128)]
    load_ve = pltpu.make_async_copy(ve_hbm.at[0], ve_own, load_sem.at[2])
    op_own = op_buf.at[pl.ds(pl.multiple_of(c * 128, 128), 128), :]
    load_op = pltpu.make_async_copy(op_hbm, op_own, load_sem.at[3])
    load_wg = pltpu.make_async_copy(wg_hbm.at[0], wg_buf, load_sem.at[4])
    load_wu = pltpu.make_async_copy(wu_hbm.at[0], wu_buf, load_sem.at[5])
    load_wd = pltpu.make_async_copy(wd_hbm.at[0], wd_buf, load_sem.at[6])
    for load in (load_q, load_cache, load_ve, load_op, load_wg, load_wu, load_wd):
        load.start()
    load_q.wait()
    load_cache.wait()

    order = onehot(
        (128, 128), lambda i: (i % 8) // 2 * 32 + (i // 8) * 2 + i % 2
    )

    def attend(t):
        query = q_buf[t]
        cache = cache_buf[t]
        scores = (
            lax.dot_general(query, cache, (((1,), (1,)), ((), ())), preferred_element_type=F32)
            * score_scale
        )
        live = lax.broadcasted_iota(jnp.int32, scores.shape, 1) < len_ref[0, t]
        top = jnp.max(jnp.where(live, scores, -1e30), axis=-1, keepdims=True)
        terms = jnp.exp(jnp.where(live, scores - top, -1e30))
        total = jnp.sum(terms, axis=-1, keepdims=True)
        latent = (dot(terms.astype(BF16), cache[:, :512]) / total).astype(BF16)
        return dot(order, latent).reshape(16, 8, 512)

    for pair in range(2):
        both = jnp.concatenate([attend(2 * pair), attend(2 * pair + 1)], axis=1)
        a2a_send[:, pair * 16 : pair * 16 + 16, :] = both.astype(BF16)

    pl.semaphore_wait(barrier, 22)

    def a2a_start(step, carry):
        p, to = zy_peer(step)
        remote(
            a2a_send.at[p], a2a_recv.at[zy], a2a_send_sem.at[step], a2a_recv_sem.at[step], to
        ).start()
        return carry

    lax.fori_loop(1, 16, a2a_start, 0)

    load_ve.wait()
    for step in range(1, 4):
        for k, core in enumerate((c, other)):
            send(
                ve_own,
                ve_own,
                ve_send_sem.at[2 * step + k],
                ve_recv_sem.at[2 * step + k],
                device((x + step) % 4, z, y, core),
            )
    send(ve_own, ve_own, ve_send_sem.at[0], ve_recv_sem.at[0], sibling)
    load_op.wait()
    send(op_own, op_own, op_send_sem.at[0], op_recv_sem.at[0], sibling)

    a2a_recv[zy] = a2a_send[zy]

    def a2a_wait(step, carry):
        _, to = zy_peer(step)
        p, _ = zy_peer(16 - step)
        copy = remote(
            a2a_send.at[zy], a2a_recv.at[p], a2a_send_sem.at[step], a2a_recv_sem.at[step], to
        )
        copy.wait_send()
        copy.wait_recv()
        return carry

    lax.fori_loop(1, 16, a2a_wait, 0)
    for step in range(1, 4):
        for k, core in enumerate((c, other)):
            arrived(
                ve_buf.at[(x + 4 - step) % 4, :, pl.ds(pl.multiple_of(core * 128, 128), 128)],
                ve_send_sem.at[2 * step + k],
                ve_recv_sem.at[2 * step + k],
            )
    arrived(
        ve_buf.at[x, :, pl.ds(pl.multiple_of(other * 128, 128), 128)],
        ve_send_sem.at[0],
        ve_recv_sem.at[0],
    )

    latents = a2a_recv[...].reshape(512, 512)
    head_of_row = lax.broadcasted_iota(jnp.int32, (512, 128), 0) % 8
    values = jnp.zeros((512, 128), F32)
    for h in range(4):
        product = dot(latents, ve_buf[h])
        values = jnp.where(head_of_row == 2 * h, product[:, :128], values)
        values = jnp.where(head_of_row == 2 * h + 1, product[:, 128:], values)
    val_f32[...] = values
    for h in range(4):
        val_send[h] = jnp.concatenate(
            [val_f32[pl.ds(2 * h, 64, stride=8), :], val_f32[pl.ds(2 * h + 1, 64, stride=8), :]],
            axis=1,
        ).astype(BF16)
    for step in range(1, 4):
        to = (x + step) % 4
        send(
            val_send.at[to],
            val_recv.at[x],
            val_send_sem.at[step],
            val_recv_sem.at[step],
            device(to, z, y, c),
        )
    val_recv[x] = val_send[x]
    arrived(
        op_buf.at[pl.ds(pl.multiple_of(other * 128, 128), 128), :],
        op_send_sem.at[0],
        op_recv_sem.at[0],
    )
    for step in range(1, 4):
        arrived(val_recv.at[(x + 4 - step) % 4], val_send_sem.at[step], val_recv_sem.at[step])

    token_order = onehot((256, 256), lambda i: (i % 16) // 4 * 64 + (i // 16) * 4 + i % 4)
    rows = dot(token_order, val_recv[...].reshape(256, 256)).astype(BF16)

    own_rows = onehot((16, 8), lambda i: jnp.where(i // 4 == x, i % 4, -1))

    p_refs = (p_a, p_b, p_c)
    r_refs = ((r1_a, r2_a, r3_a), (r1_b, r2_b, r3_b), (r1_c, r2_c, r3_c))
    s_refs = ((s1_a, s2_a), (s1_b, s2_b), (s1_c, s2_c))
    n_refs = (n_a, n_b, n_c)

    def slot(round_, part, phase, step):
        return ((round_ * 3 + part) * 3 + phase) * 4 + step

    def left_axes(part, phase):
        done = PARTS[part][2][:phase]
        return [a for a in (0, 1, 2) if a not in done]

    def rs_source(part, phase):
        return p_refs[part] if phase == 0 else s_refs[part][phase - 1]

    def block(part, phase, index):
        axis = PARTS[part][2][phase]
        return tuple(index if a == axis else slice(None) for a in left_axes(part, phase))

    def rs_send(round_, part, phase):
        axis = PARTS[part][2][phase]
        for step in range(1, 4):
            s = slot(round_, part, phase, step)
            send(
                rs_source(part, phase).at[block(part, phase, (here[axis] + step) % 4)],
                r_refs[part][phase].at[step - 1],
                rs_send_sem.at[s],
                rs_recv_sem.at[s],
                peer(axis, step),
            )

    def rs_wait(round_, part, phase):
        for step in range(1, 4):
            s = slot(round_, part, phase, step)
            arrived(r_refs[part][phase].at[step - 1], rs_send_sem.at[s], rs_recv_sem.at[s])

    def rs_sum(part, phase):
        axis = PARTS[part][2][phase]
        source = rs_source(part, phase).at[block(part, phase, here[axis])]
        received = r_refs[part][phase]

        def total(*at):
            value = source[at].astype(F32)
            for k in range(3):
                value = value + received[(k, *at)].astype(F32)
            return value

        if phase == 2:
            return total()
        target = s_refs[part][phase]

        def add(i, carry):
            if phase == 1:
                target[i] = total(i).astype(BF16)
            else:
                for j in range(4):
                    target[i, j] = total(i, j).astype(BF16)
            return carry

        lax.fori_loop(0, 4, add, 0)
        return None

    def reduce_rows(round_, finish):
        for phase in range(3):
            for part in range(3):
                rs_wait(round_, part, phase)
                result = rs_sum(part, phase)
                if phase < 2:
                    rs_send(round_, part, phase + 1)
                else:
                    finish(part, result)

    residual = res_ref[...]
    for part, (offset, width, _) in enumerate(PARTS):

        def project(k, carry, part=part, offset=offset, width=width):
            columns = pl.ds(pl.multiple_of(k * QUARTER + offset, 128), width)
            p_refs[part][k] = dot(rows, op_buf[:, columns]).astype(BF16).reshape(4, 4, 16, width)
            own = p_refs[part].at[k, z, y]
            own[...] = (own[...].astype(F32) + dot(own_rows, res_ref[:, columns])).astype(BF16)
            return carry

        lax.fori_loop(0, 4, project, 0)
        rs_send(0, part, 0)

    lane = lax.broadcasted_iota(jnp.int32, (8, 128), 1)
    table = jnp.zeros((8, 128), F32)
    for k in range(8):
        table = table + jnp.where(ids_ref[:, k : k + 1] == lane, gates_ref[:, k : k + 1], 0.0)
    table = dot(own_rows, table.astype(BF16))

    squares = []

    def keep_stream(part, result):
        offset, width, _ = PARTS[part]
        stream_buf[:, offset : offset + width] = result
        squares.append(jnp.sum(result * result, axis=-1, keepdims=True))
        columns = pl.ds(pl.multiple_of(x * QUARTER + offset, 128), width)
        n_refs[part][c, x, z, y, :, :width] = (result * gain_ref[:, columns].astype(F32)).astype(
            BF16
        )

    reduce_rows(0, keep_stream)
    square = squares[0] + squares[1] + squares[2]
    high = square.astype(BF16).astype(F32)
    lane16 = lax.broadcasted_iota(jnp.int32, (16, 128), 1)
    extra = jnp.where(lane16 == 32, high, jnp.where(lane16 == 33, square - high, table))
    n_c[c, x, z, y, :, 512:] = extra.astype(BF16)

    def ag_block(part, phase, index):
        axes = PARTS[part][2]
        at = [slice(None)] * 3
        for a in axes[:phase]:
            at[a] = here[a]
        at[axes[phase]] = index
        return n_refs[part].at[(c, *at)]

    for phase in (2, 1, 0):
        for part in range(3):
            axis = PARTS[part][2][phase]
            if phase < 2:
                before = PARTS[part][2][phase + 1]
                for step in range(1, 4):
                    s = slot(0, part, phase + 1, step)
                    arrived(
                        ag_block(part, phase + 1, (here[before] + 4 - step) % 4),
                        ag_send_sem.at[s],
                        ag_recv_sem.at[s],
                    )
            for step in range(1, 4):
                s = slot(0, part, phase, step)
                own = ag_block(part, phase, here[axis])
                send(own, own, ag_send_sem.at[s], ag_recv_sem.at[s], peer(axis, step))
    for part in range(3):
        axis = PARTS[part][2][0]
        for step in range(1, 4):
            s = slot(0, part, 0, step)
            arrived(
                ag_block(part, 0, (here[axis] + 4 - step) % 4),
                ag_send_sem.at[s],
                ag_recv_sem.at[s],
            )
        half = n_refs[part].at[c]
        send(half, half, pair_send_sem.at[part], pair_recv_sem.at[part], sibling)

    load_wg.wait()
    load_wu.wait()
    load_wd.wait()
    expert = z * 8 + y * 2 + c
    lanes = lax.broadcasted_iota(jnp.int32, (256, 128), 1)
    for half, core in enumerate((c, other)):
        if half == 1:
            for part in range(3):
                arrived(n_refs[part].at[core], pair_send_sem.at[part], pair_recv_sem.at[part])
        acc_g[...] = jnp.zeros_like(acc_g)
        acc_u[...] = jnp.zeros_like(acc_u)
        for part, (offset, width, _) in enumerate(PARTS):

            def up(k, carry, part=part, offset=offset, width=width, core=core):
                chunk = n_refs[part][core, k, :, :, :, :width].reshape(256, width)
                depth = pl.ds(pl.multiple_of(k * QUARTER + offset, 128), width)
                acc_g[...] += dot(chunk, wg_buf[depth, :])
                acc_u[...] += dot(chunk, wu_buf[depth, :])
                return carry

            lax.fori_loop(0, 4, up, 0)
        extra = jnp.zeros((256, 128), F32)
        for k in range(4):
            extra = extra + n_c[core, k, :, :, :, 512:].reshape(256, 128).astype(F32)
        weight = jnp.sum(jnp.where(lanes == expert, extra, 0.0), axis=-1, keepdims=True)
        square = jnp.sum(
            jnp.where((lanes == 32) | (lanes == 33), extra, 0.0), axis=-1, keepdims=True
        )
        scale = lax.rsqrt(square * (1.0 / D) + norm_eps)
        gate = acc_g[...] * scale
        act = gate / (1.0 + jnp.exp(-gate)) * (acc_u[...] * scale)
        act_buf[half] = (act * weight).astype(BF16)

    for copy in sends:
        copy.wait_send()
    sends.clear()

    far_refs = (far_a, far_b, far_c)
    for part, (offset, width, _) in enumerate(PARTS):

        def down_far(k, carry, part=part, offset=offset, width=width):
            columns = pl.ds(pl.multiple_of(k * QUARTER + offset, 128), width)
            n_refs[part][c, k, :, :, :, :width] = (
                dot(act_buf[1], wd_buf[:, columns]).astype(BF16).reshape(4, 4, 16, width)
            )
            return carry

        lax.fori_loop(0, 4, down_far, 0)
        send(
            n_refs[part].at[c, :, :, :, :, pl.ds(0, width)],
            far_refs[part],
            far_send_sem.at[part],
            far_recv_sem.at[part],
            sibling,
        )
    for part, (offset, width, _) in enumerate(PARTS):
        arrived(far_refs[part], far_send_sem.at[part], far_recv_sem.at[part])

        def down(k, carry, part=part, offset=offset, width=width):
            columns = pl.ds(pl.multiple_of(k * QUARTER + offset, 128), width)
            total = dot(act_buf[0], wd_buf[:, columns])
            total = total + far_refs[part][k].reshape(256, width).astype(F32)
            p_refs[part][k] = total.astype(BF16).reshape(4, 4, 16, width)
            return carry

        lax.fori_loop(0, 4, down, 0)
        rs_send(1, part, 0)

    def add_stream(part, result):
        offset, width, _ = PARTS[part]
        stream_buf[:, offset : offset + width] += result

    reduce_rows(1, add_stream)

    rounded = stream_buf[...].astype(BF16)
    last = jnp.zeros((64, 512), F32)
    for j in range(4):
        pick = onehot(
            (64, 16), lambda i: jnp.where((i % 16) // 4 == j, i // 16 * 4 + i % 4, -1)
        )
        piece = rounded[:, j * 512 : min(j * 512 + 512, QUARTER)]
        moved = dot(pick, piece)
        if moved.shape[1] < 512:
            moved = jnp.concatenate([moved, jnp.zeros((64, 512 - moved.shape[1]), F32)], axis=1)
        last = last + moved
    last_send[...] = last.astype(BF16).reshape(4, 16, 512)
    for step in range(1, 4):
        to = (x + step) % 4
        send(
            last_send.at[to],
            out_ref.at[x],
            last_send_sem.at[step],
            last_recv_sem.at[step],
            device(to, z, y, c),
        )
    out_ref[x] = last_send[x]
    for step in range(1, 4):
        arrived(out_ref.at[(x + 4 - step) % 4], last_send_sem.at[step], last_recv_sem.at[step])
    for copy in sends:
        copy.wait_send()


def per_device(
    queries,
    compressed_cache,
    lengths,
    value_expand_matrix,
    out_proj,
    residual,
    norm_gain,
    expert_ids,
    expert_gates,
    w_gate,
    w_up,
    w_down,
):
    vmem = lambda *shape, dtype=BF16: pltpu.VMEM(shape, dtype)
    widths = [w for _, w, _ in PARTS]
    dma = lambda n: pltpu.SemaphoreType.DMA((n,))
    scratch = [
        vmem(4, 128, 576),
        vmem(4, 512, 576),
        vmem(256, D),
        vmem(D, 512),
        vmem(D, 512),
        vmem(512, D),
        vmem(4, 512, 256),
        vmem(16, 32, 512),
        vmem(16, 32, 512),
        vmem(512, 128, dtype=F32),
        vmem(4, 64, 256),
        vmem(4, 64, 256),
        *[vmem(4, 4, 4, 16, w) for w in widths],
        *[vmem(3, 4, 4, 16, w) for w in widths],
        *[vmem(4, 4, 16, w) for w in widths],
        *[vmem(3, 4, 16, w) for w in widths],
        *[vmem(4, 16, w) for w in widths],
        *[vmem(3, 16, w) for w in widths],
        *[vmem(2, 4, 4, 4, 16, WIDE) for w in widths],
        vmem(16, QUARTER, dtype=F32),
        vmem(256, 512, dtype=F32),
        vmem(256, 512, dtype=F32),
        vmem(2, 256, 512),
        *[vmem(4, 4, 4, 16, w) for w in widths],
        vmem(4, 16, 512),
        dma(7),
        dma(8),
        dma(8),
        dma(1),
        dma(1),
        dma(16),
        dma(16),
        dma(4),
        dma(4),
        dma(72),
        dma(72),
        dma(36),
        dma(36),
        dma(3),
        dma(3),
        dma(3),
        dma(3),
        dma(4),
        dma(4),
    ]
    in_vmem = pl.BlockSpec(memory_space=pltpu.VMEM)
    anywhere = pl.BlockSpec(memory_space=pl.ANY)
    pad = lambda a: jnp.concatenate([a, jnp.zeros_like(a)], axis=0)
    result = pl.pallas_call(
        kernel,
        out_shape=jax.ShapeDtypeStruct((4, 16, 512), BF16),
        in_specs=[pl.BlockSpec(memory_space=pltpu.SMEM)] + [in_vmem] * 4 + [anywhere] * 7,
        out_specs=in_vmem,
        scratch_shapes=scratch,
        compiler_params=pltpu.CompilerParams(
            collective_id=0, has_side_effects=True, vmem_limit_bytes=64 << 20
        ),
        cost_estimate=pl.CostEstimate(
            flops=14 * 10**9, bytes_accessed=28 * 10**6, transcendentals=600_000
        ),
        name="layer",
    )(
        lengths,
        pad(residual[0]),
        norm_gain[None],
        pad(expert_ids[0]),
        pad(expert_gates[0].astype(F32)),
        queries,
        compressed_cache,
        value_expand_matrix,
        out_proj,
        w_gate,
        w_up,
        w_down,
    )
    result = result.reshape(4, 4, 4, 512).transpose(2, 0, 1, 3).reshape(4, 4, 2048)
    return result[:, :, :QUARTER].reshape(1, 4, D)


def solution(mesh):
    in_specs = (
        P("grp", "role", None, None),
        P("grp", "role", None, None),
        P("grp", "role"),
        P(("role", "grp"), None, None),
        P(("role", "grp"), None),
        P("grp", "role", None),
        P(),
        P("grp", "role", None),
        P("grp", "role", None),
        P("grp", None, "role"),
        P("grp", None, "role"),
        P("grp", "role", None),
    )
    out_specs = P("grp", "role", None)
    return jax.shard_map(
        per_device, mesh=mesh, in_specs=in_specs, out_specs=out_specs, check_vma=False
    )
```

time: 443 us -> 154 us (0.35)
  waiting for transfers between devices: 274 us -> 0 us
  Pallas kernels: 0 us -> 140 us
  blocking collectives: 95.4 us -> 0 us
  matrix products: 31.9 us -> 0 us
  between operations: 13.6 us -> 0.03 us
  starting transfers between devices: 7.42 us -> 0 us
  local copies, waits for them, and re-layouts: 17.2 us -> 12.2 us
    unnamed x3 -> x0, waiting for transfers between devices: 161 us -> none
    pallas_call x0 -> x1, Pallas kernels: none -> 140 us  [per_device(): pl.pallas_call(kernel, out_shape=jax.ShapeDtypeStruct((4, 16, 512), BF16)...]
    all_to_all x2 -> x0, blocking collectives: 75.1 us -> none  [the longest x1 50.6 us: per_device(): lax.all_to_all(send_rows, 'grp', split_axis=0, concat_axis=0, tiled=True)]
    psum x1 -> x0, waiting for transfers between devices: 65.5 us -> none  [per_device(): lax.psum(partial_value.astype(jnp.bfloat16), 'role').astype(jnp.float32)]
    all_to_all x1 -> x0, waiting for transfers between devices: 47.6 us -> none  [per_device(): lax.all_to_all(full_sum.astype(jnp.bfloat16), 'grp', split_axis=0, concat...]
    dot_general x8 -> x0, matrix products: 31.9 us -> none  [the longest x1 6.46 us: per_device(): jnp.dot(value_rows.reshape(tok_here * lax.axis_size(('role', 'grp')), -1)...]
    all_gather x2 -> x0, blocking collectives: 20.3 us -> none  [the longest x1 12.2 us: per_device(): lax.all_gather(normed[None], 'role', axis=1, tiled=True)]
    all_to_all x1 -> x0, starting transfers between devices: 7.38 us -> none  [per_device(): lax.all_to_all(full_sum.astype(jnp.bfloat16), 'grp', split_axis=0, concat...]
  transfers between devices with their start and end apart: 3 -> 0, of which waited for: 3 -> 0; matrix products, arithmetic and copies ran while one was open for 0% -> 0% of each run, Pallas kernels for 0% -> 0%
where the time goes in v1:
time: 154 us; the launch traced here: 153 us
  Pallas kernels  140 us (91%)
  local copies, waits for them, and re-layouts  12.2 us (8%)
    pallas_call x1, Pallas kernels, per_device(): pl.pallas_call(kernel, out_shape=jax.ShapeDtypeStruct((4, 16, 512), BF16)...  140 us
    unnamed x2, local copies, waits for them, and re-layouts  6.48 us

profile of v1, /device:TPU:0, one launch (start us, length us, event | category | flops | bytes accessed | tf_op | source)
XLA Modules:
  0.0 153.1 jit_solution(14451020064030926786)
XLA Ops:
  0.0 1.3 concatenate.12.ids_ref
  1.3 1.3 pad_convert_fusion.gates_ref
  2.5 1.3 broadcast_in_dim.2.gain_ref
  3.9 1.5 concatenate.11.res_ref
  5.4 2.1 %copy.15.q_hbm = bf16[1,4,128,576]{3,2,1,0:T(8,128)(2,1)} copy(bf16[1,4,128,576]{2,3,1,0:T(8,128)(2,1)} %param.12) | data formatting | bytes 1179648 | tf_op args[0]
  7.5 4.3 %copy.16.cache_hbm = bf16[1,4,512,576]{3,2,1,0:T(8,128)(2,1)} copy(bf16[1,4,512,576]{2,3,1,0:T(8,128)(2,1)} %param.13) | data formatting | bytes 4718592 | tf_op args[1]
  11.8 139.6 %layer.1 = bf16[4,16,512]{2,1,0:T(8,128)(2,1)} custom-call(s32[1,4]{1,0:T(1,128)} %len_ref.1, bf16[8,7168]{1,0:T(8,128)(2,1)} %concatenate.11.res_ref, bf16[1,7168]{1,0:T(2,128)(2,1)} %broadcast_in_dim.2.gain_ref, s32[8,8]{1,0:T(8,128)} %concatenate.12.ids_ref, f32[8,8]{1,0:T(8,128)} %pad_convert_fusion.gates_ref, bf16[1,4,128,576]{3,2,1,0:T(8,128)(2,1)} %copy.15.q_hbm, ...), custom_call_target="tpu_custom_call" | custom-call | flops 14000000000 | bytes 28000000 | tf_op jit(solution)/shard_map/layer/pallas_call | solution.py:605
  151.5 0.9 reshape.11
  152.5 0.6 reshape.13
  (3 shorter events, 0.1 us)

commit v2 on v1

v2 whole, which is shorter than its diff:
```python
import jax
import jax.numpy as jnp
from jax import lax
from jax.experimental import pallas as pl
from jax.experimental.pallas import tpu as pltpu
from jax.sharding import PartitionSpec as P

MESH = pl.DeviceIdType.MESH
F32 = jnp.float32
BF16 = jnp.bfloat16

score_scale = 192.0 ** (-0.5)
norm_eps = 1e-06

D = 7168
QUARTER = 1792
FLOWS = (
    (0, 384, (0, 1, 2)),
    (384, 256, (1, 2, 0)),
    (640, 256, (2, 0, 1)),
    (896, 256, (0, 1, 2)),
    (1152, 384, (1, 2, 0)),
    (1536, 256, (2, 0, 1)),
)
LAST = 5
SETS = ((0, 1, 2), (3, 4, 5))
LAG = 2
FLOW = object()


def coordinates():
    grp = lax.axis_index("grp")
    return lax.axis_index("role"), grp // 8, (grp // 2) % 4, grp % 2


def device(x, z, y, c):
    return {"role": x, "grp": z * 8 + y * 2 + c}


def dot(a, b):
    return jnp.dot(a, b, preferred_element_type=F32)


def onehot(shape, source_of_row):
    rows = lax.broadcasted_iota(jnp.int32, shape, 0)
    columns = lax.broadcasted_iota(jnp.int32, shape, 1)
    return (columns == source_of_row(rows)).astype(BF16)


def kernel(
    len_ref,
    res_ref,
    gain_ref,
    ids_ref,
    gates_ref,
    q_hbm,
    cache_hbm,
    ve_hbm,
    op_hbm,
    wg_hbm,
    wu_hbm,
    wd_hbm,
    out_ref,
    q_buf,
    cache_buf,
    op_buf,
    wg_buf,
    wu_buf,
    wd_buf,
    ve_buf,
    a2a_send,
    a2a_recv,
    gain_f32,
    val_f32,
    val_send,
    val_recv,
    p_refs,
    x_refs,
    y_refs,
    s1_refs,
    r2_refs,
    s2_refs,
    r3_refs,
    n_refs,
    stream_buf,
    acc_g,
    acc_u,
    act_buf,
    far_refs,
    last_send,
    load_sem,
    ve_send_sem,
    ve_recv_sem,
    op_send_sem,
    op_recv_sem,
    a2a_send_sem,
    a2a_recv_sem,
    val_send_sem,
    val_recv_sem,
    rs_send_sem,
    rs_recv_sem,
    ag_send_sem,
    ag_recv_sem,
    pair_send_sem,
    pair_recv_sem,
    far_send_sem,
    far_recv_sem,
    last_send_sem,
    last_recv_sem,
):
    x, z, y, c = coordinates()
    zy = z * 4 + y
    other = 1 - c
    here = (x, z, y)
    me = device(x, z, y, c)
    sibling = device(x, z, y, other)
    sends = []

    def peer(axis, step):
        at = [x, z, y]
        at[axis] = (at[axis] + step) % 4
        return device(at[0], at[1], at[2], c)

    def remote(src, dst, send_sem, recv_sem, to):
        return pltpu.make_async_remote_copy(
            src_ref=src,
            dst_ref=dst,
            send_sem=send_sem,
            recv_sem=recv_sem,
            device_id=to,
            device_id_type=MESH,
        )

    def send(src, dst, send_sem, recv_sem, to):
        copy = remote(src, dst, send_sem, recv_sem, to)
        copy.start()
        sends.append(copy)

    def arrived(dst, send_sem, recv_sem):
        remote(dst, dst, send_sem, recv_sem, me).wait_recv()

    def zy_peer(step):
        p = (zy + step) % 16
        return p, device(x, p // 4, p % 4, c)

    barrier = pltpu.get_barrier_semaphore()

    def greet(step, carry):
        _, to = zy_peer(step)
        pl.semaphore_signal(barrier, inc=1, device_id=to, device_id_type=MESH)
        return carry

    lax.fori_loop(1, 16, greet, 0)
    for step in range(1, 4):
        for core in (c, other):
            pl.semaphore_signal(
                barrier, inc=1, device_id=device((x + step) % 4, z, y, core), device_id_type=MESH
            )
    pl.semaphore_signal(barrier, inc=1, device_id=sibling, device_id_type=MESH)

    ve_own = ve_buf.at[x, :, pl.ds(pl.multiple_of(c * 128, 128), 128)]
    op_own = op_buf.at[pl.ds(pl.multiple_of(c * 128, 128), 128), :]
    load_tokens = []
    for pair in range(2):
        rows = pl.ds(2 * pair, 2)
        load_tokens.append(
            (
                pltpu.make_async_copy(q_hbm.at[0, rows], q_buf.at[rows], load_sem.at[2 * pair]),
                pltpu.make_async_copy(
                    cache_hbm.at[0, rows], cache_buf.at[rows], load_sem.at[2 * pair + 1]
                ),
            )
        )
    load_ve = pltpu.make_async_copy(ve_hbm.at[0], ve_own, load_sem.at[4])
    load_op = pltpu.make_async_copy(op_hbm, op_own, load_sem.at[5])
    load_wg = pltpu.make_async_copy(wg_hbm.at[0], wg_buf, load_sem.at[6])
    load_wu = pltpu.make_async_copy(wu_hbm.at[0], wu_buf, load_sem.at[7])
    load_wd = pltpu.make_async_copy(wd_hbm.at[0], wd_buf, load_sem.at[8])
    for load in (*load_tokens[0], *load_tokens[1], load_ve, load_op):
        load.start()

    gain_f32[...] = gain_ref[...].astype(F32).reshape(1, D)

    order = onehot((128, 128), lambda i: (i % 8) // 2 * 32 + (i // 8) * 2 + i % 2)

    def attend(t):
        query = q_buf[t]
        cache = cache_buf[t]
        scores = (
            lax.dot_general(query, cache, (((0,), (0,)), ((), ())), preferred_element_type=F32)
            * score_scale
        )
        live = lax.broadcasted_iota(jnp.int32, scores.shape, 1) < len_ref[0, t]
        top = jnp.max(jnp.where(live, scores, -1e30), axis=-1, keepdims=True)
        terms = jnp.exp(jnp.where(live, scores - top, -1e30))
        total = jnp.sum(terms, axis=-1, keepdims=True)
        latent = lax.dot_general(
            terms.astype(BF16),
            cache[:512],
            (((1,), (1,)), ((), ())),
            preferred_element_type=F32,
        )
        latent = (latent / total).astype(BF16)
        return dot(order, latent).reshape(16, 8, 512)

    def attend_pair(pair):
        for load in load_tokens[pair]:
            load.wait()
        both = jnp.concatenate([attend(2 * pair), attend(2 * pair + 1)], axis=1)
        a2a_send[pair] = both.astype(BF16)

    def a2a_start(pair):
        def start(step, carry):
            p, to = zy_peer(step)
            remote(
                a2a_send.at[pair, p],
                a2a_recv.at[pair, zy],
                a2a_send_sem.at[pair, step],
                a2a_recv_sem.at[pair, step],
                to,
            ).start()
            return carry

        lax.fori_loop(1, 16, start, 0)
        a2a_recv[pair, zy] = a2a_send[pair, zy]

    def a2a_wait(pair):
        def wait(step, carry):
            p, to = zy_peer(16 - step)
            copy = remote(
                a2a_send.at[pair, zy],
                a2a_recv.at[pair, p],
                a2a_send_sem.at[pair, step],
                a2a_recv_sem.at[pair, step],
                to,
            )
            copy.wait_send()
            copy.wait_recv()
            return carry

        lax.fori_loop(1, 16, wait, 0)

    attend_pair(0)
    for load in (load_wg, load_wu, load_wd):
        load.start()
    pl.semaphore_wait(barrier, 22)
    a2a_start(0)

    load_ve.wait()
    for step in range(1, 4):
        send(
            ve_own,
            ve_own,
            ve_send_sem.at[step],
            ve_recv_sem.at[step],
            device((x + step) % 4, z, y, c),
        )
    load_op.wait()
    send(op_own, op_own, op_send_sem.at[0], op_recv_sem.at[0], sibling)

    attend_pair(1)
    a2a_start(1)
    for step in range(1, 4):
        arrived(
            ve_buf.at[(x + 4 - step) % 4, :, pl.ds(pl.multiple_of(c * 128, 128), 128)],
            ve_send_sem.at[step],
            ve_recv_sem.at[step],
        )
    ve_ring = ve_buf.at[:, :, pl.ds(pl.multiple_of(c * 128, 128), 128)]
    send(ve_ring, ve_ring, ve_send_sem.at[0], ve_recv_sem.at[0], sibling)
    a2a_wait(0)
    a2a_wait(1)
    arrived(
        ve_buf.at[:, :, pl.ds(pl.multiple_of(other * 128, 128), 128)],
        ve_send_sem.at[0],
        ve_recv_sem.at[0],
    )

    latents = a2a_recv[...].reshape(512, 512)
    head_of_row = lax.broadcasted_iota(jnp.int32, (512, 128), 0) % 8
    values = jnp.zeros((512, 128), F32)
    for h in range(4):
        product = dot(latents, ve_buf[h])
        values = jnp.where(head_of_row == 2 * h, product[:, :128], values)
        values = jnp.where(head_of_row == 2 * h + 1, product[:, 128:], values)
    val_f32[...] = values
    for h in range(4):
        val_send[h] = jnp.concatenate(
            [val_f32[pl.ds(2 * h, 64, stride=8), :], val_f32[pl.ds(2 * h + 1, 64, stride=8), :]],
            axis=1,
        ).astype(BF16)
    for step in range(1, 4):
        to = (x + step) % 4
        send(
            val_send.at[to],
            val_recv.at[x],
            val_send_sem.at[step],
            val_recv_sem.at[step],
            device(to, z, y, c),
        )
    val_recv[x] = val_send[x]
    arrived(
        op_buf.at[pl.ds(pl.multiple_of(other * 128, 128), 128), :],
        op_send_sem.at[0],
        op_recv_sem.at[0],
    )
    for step in range(1, 4):
        arrived(val_recv.at[(x + 4 - step) % 4], val_send_sem.at[step], val_recv_sem.at[step])

    token_order = onehot((256, 256), lambda i: (i % 16) // 4 * 64 + (i % 4) // 2 * 32 + (i // 16) * 2 + i % 2)
    rows = dot(token_order, val_recv[...].reshape(256, 256)).astype(BF16)

    own_rows = onehot((16, 4), lambda i: jnp.where(i // 4 == x, i % 4, -1))

    halves = (pl.ds(0, 2), pl.ds(2, 2))

    def ring_block(flow, index, half):
        at = [slice(None)] * 3
        first = FLOWS[flow][2][0]
        at[first] = index
        if half is not None:
            at[1 if first == 0 else 0] = halves[half]
        return tuple(at)

    def rs_sem(round_, flow, k):
        s = (round_ * 6 + flow) * 12 + k
        return rs_send_sem.at[s], rs_recv_sem.at[s]

    def ring_at(flow, step):
        return (here[FLOWS[flow][2][0]] + step) % 4

    def ring_start(round_, flow):
        axis = FLOWS[flow][2][0]
        p = p_refs[flow]
        for k, (step, block, half) in enumerate(((1, 2, 0), (3, 2, 1))):
            send(
                p.at[ring_block(flow, ring_at(flow, block), half)],
                x_refs[flow].at[k],
                *rs_sem(round_, flow, k),
                peer(axis, step),
            )
        for k, (step, half) in enumerate(((1, 1), (3, 0))):
            send(
                p.at[ring_block(flow, ring_at(flow, step), half)],
                y_refs[flow].at[k, halves[half]],
                *rs_sem(round_, flow, 2 + k),
                peer(axis, step),
            )

    def ring_pass(round_, flow):
        axis = FLOWS[flow][2][0]
        p = p_refs[flow]
        for k, (step, half) in enumerate(((1, 0), (3, 1))):
            arrived(x_refs[flow].at[k], *rs_sem(round_, flow, k))
            own = p.at[ring_block(flow, ring_at(flow, step), half)]

            def add(i, carry, own=own, k=k):
                own[i] = (own[i].astype(F32) + x_refs[flow][k, i].astype(F32)).astype(BF16)
                return carry

            lax.fori_loop(0, 2, add, 0)
            send(
                own,
                y_refs[flow].at[k, halves[half]],
                *rs_sem(round_, flow, 4 + k),
                peer(axis, step),
            )

    def ring_end(round_, flow):
        for k, half in ((0, 1), (1, 0)):
            arrived(y_refs[flow].at[k, halves[half]], *rs_sem(round_, flow, 2 + k))
        for k, half in ((0, 0), (1, 1)):
            arrived(y_refs[flow].at[k, halves[half]], *rs_sem(round_, flow, 4 + k))
        own = p_refs[flow].at[ring_block(flow, ring_at(flow, 0), None)]
        y_ref = y_refs[flow]

        def add(i, carry):
            total = own[i].astype(F32) + y_ref[0, i].astype(F32) + y_ref[1, i].astype(F32)
            s1_refs[flow][i] = total.astype(BF16)
            return carry

        lax.fori_loop(0, 4, add, 0)
        direct_start(round_, flow, 1)

    def direct_block(flow, phase, index):
        if phase == 2:
            return s2_refs[flow].at[index]
        _, axis, last = FLOWS[flow][2]
        return s1_refs[flow].at[(index,) if axis < last else (slice(None), index)]

    def direct_start(round_, flow, phase):
        axis = FLOWS[flow][2][phase]
        received = (r2_refs if phase == 1 else r3_refs)[flow]
        for step in range(1, 4):
            send(
                direct_block(flow, phase, (here[axis] + step) % 4),
                received.at[step - 1],
                *rs_sem(round_, flow, 3 + 3 * phase + step - 1),
                peer(axis, step),
            )

    def direct_end(round_, flow, phase):
        axis = FLOWS[flow][2][phase]
        received = (r2_refs if phase == 1 else r3_refs)[flow]
        for step in range(1, 4):
            arrived(received.at[step - 1], *rs_sem(round_, flow, 3 + 3 * phase + step - 1))
        total = direct_block(flow, phase, here[axis])[...].astype(F32)
        for k in range(3):
            total = total + received[k].astype(F32)
        if phase == 2:
            return total
        s2_refs[flow][...] = total.astype(BF16)
        direct_start(round_, flow, 2)
        return None

    def project(flow):
        offset, width, _ = FLOWS[flow]

        def chunk(k, carry):
            columns = pl.ds(pl.multiple_of(k * QUARTER + offset, 128), width)
            p_refs[flow][k] = dot(rows, op_buf[:, columns]).astype(BF16).reshape(4, 4, 16, width)
            own = p_refs[flow].at[k, z, y]
            own[...] = (own[...].astype(F32) + dot(own_rows, res_ref[:, columns])).astype(BF16)
            return carry

        lax.fori_loop(0, 4, chunk, 0)
        ring_start(0, flow)

    squares = []

    def keep_stream(flow):
        offset, width, _ = FLOWS[flow]
        result = direct_end(0, flow, 2)
        stream_buf[:, offset : offset + width] = result
        squares.append(jnp.sum(result * result, axis=-1, keepdims=True))
        columns = pl.ds(pl.multiple_of(x * QUARTER + offset, 128), width)
        n_refs[flow][c, x, z, y, :, :width] = (result * gain_f32[:, columns]).astype(BF16)
        if flow == LAST:
            lane = lax.broadcasted_iota(jnp.int32, (4, 128), 1)
            table = jnp.zeros((4, 128), F32)
            gates = gates_ref[...].astype(F32)
            for k in range(8):
                table = table + jnp.where(ids_ref[:, k : k + 1] == lane, gates[:, k : k + 1], 0.0)
            table = dot(own_rows, table.astype(BF16))
            square = sum(squares)
            high = square.astype(BF16).astype(F32)
            lane16 = lax.broadcasted_iota(jnp.int32, (16, 128), 1)
            extra = jnp.where(lane16 == 32, high, jnp.where(lane16 == 33, square - high, table))
            n_refs[flow][c, x, z, y, :, width:] = extra.astype(BF16)
        ag_start(flow, 2)

    def ag_sem(flow, k):
        s = flow * 12 + k
        return ag_send_sem.at[s], ag_recv_sem.at[s]

    def ag_block(flow, phase, index):
        axes = FLOWS[flow][2]
        at = [slice(None)] * 3
        for a in axes[:phase]:
            at[a] = here[a]
        at[axes[phase]] = index
        return n_refs[flow].at[(c, *at)]

    def ag_start(flow, phase):
        axis = FLOWS[flow][2][phase]
        own = ag_block(flow, phase, here[axis])
        for step in range(1, 4):
            send(own, own, *ag_sem(flow, 3 + 3 * phase + step - 1), peer(axis, step))

    def ag_end(flow, phase):
        axis = FLOWS[flow][2][phase]
        for step in range(1, 4):
            arrived(
                ag_block(flow, phase, (here[axis] + 4 - step) % 4),
                *ag_sem(flow, 3 + 3 * phase + step - 1),
            )
        if phase == 2:
            ag_start(flow, 1)
        else:
            for k, (step, half) in enumerate(((1, 0), (3, 1), (1, 1), (3, 0))):
                own = n_refs[flow].at[(c, *ring_block(flow, ring_at(flow, 0), half))]
                send(own, own, *ag_sem(flow, k), peer(FLOWS[flow][2][0], step))

    def ag_pass(flow):
        for k, (step, half) in enumerate(((1, 0), (3, 1))):
            got = n_refs[flow].at[(c, *ring_block(flow, ring_at(flow, 4 - step), half))]
            arrived(got, *ag_sem(flow, k))
            send(got, got, *ag_sem(flow, 4 + k), peer(FLOWS[flow][2][0], step))

    def ag_last(flow):
        for k, (step, half) in enumerate(((1, 1), (3, 0))):
            got = n_refs[flow].at[(c, *ring_block(flow, ring_at(flow, 4 - step), half))]
            arrived(got, *ag_sem(flow, 2 + k))
        for k, half in enumerate((0, 1)):
            got = n_refs[flow].at[(c, *ring_block(flow, ring_at(flow, 2), half))]
            arrived(got, *ag_sem(flow, 4 + k))
        half = n_refs[flow].at[c]
        send(half, half, pair_send_sem.at[flow], pair_recv_sem.at[flow], sibling)

    def up(flow, half):
        offset, width, _ = FLOWS[flow]
        core = (c, other)[half]
        if half == 1:
            arrived(n_refs[flow].at[core], pair_send_sem.at[flow], pair_recv_sem.at[flow])
        if flow == 0:
            if half == 0:
                load_wg.wait()
                load_wu.wait()
            acc_g[half] = jnp.zeros((256, 512), F32)
            acc_u[half] = jnp.zeros((256, 512), F32)

        def chunk(k, carry):
            rows = n_refs[flow][core, k, :, :, :, :width].reshape(256, width)
            depth = pl.ds(pl.multiple_of(k * QUARTER + offset, 128), width)
            acc_g[half] += dot(rows, wg_buf[depth, :])
            acc_u[half] += dot(rows, wu_buf[depth, :])
            return carry

        lax.fori_loop(0, 4, chunk, 0)

    expert = z * 8 + y * 2 + c
    lanes = lax.broadcasted_iota(jnp.int32, (256, 128), 1)

    def activate(half):
        core = (c, other)[half]
        extra = jnp.zeros((256, 128), F32)
        for k in range(4):
            extra = extra + n_refs[LAST][core, k, :, :, :, 256:].reshape(256, 128).astype(F32)
        weight = jnp.sum(jnp.where(lanes == expert, extra, 0.0), axis=-1, keepdims=True)
        square = jnp.sum(
            jnp.where((lanes == 32) | (lanes == 33), extra, 0.0), axis=-1, keepdims=True
        )
        scale = lax.rsqrt(square * (1.0 / D) + norm_eps)
        gate = acc_g[half] * scale
        act = gate / (1.0 + jnp.exp(-gate)) * (acc_u[half] * scale)
        act_buf[half] = (act * weight).astype(BF16)

    def each(function, *arguments):
        def run(number):
            for flow in SETS[number]:
                function(*(flow if a is FLOW else a for a in arguments))

        return run

    first = (
        each(project, FLOW),
        each(ring_pass, 0, FLOW),
        each(ring_end, 0, FLOW),
        each(direct_end, 0, FLOW, 1),
        each(keep_stream, FLOW),
        each(ag_end, FLOW, 2),
        each(ag_end, FLOW, 1),
        each(ag_pass, FLOW),
        each(ag_last, FLOW),
        each(up, FLOW, 0),
        each(up, FLOW, 1),
    )
    for tick in range(len(first) + LAG):
        if tick < len(first):
            first[tick](0)
        if tick >= LAG:
            first[tick - LAG](1)
    activate(1)
    activate(0)

    for copy in sends:
        copy.wait_send()
    sends.clear()

    load_wd.wait()

    def down_far(flow):
        offset, width, _ = FLOWS[flow]

        def chunk(k, carry):
            columns = pl.ds(pl.multiple_of(k * QUARTER + offset, 128), width)
            n_refs[flow][c, k, :, :, :, :width] = (
                dot(act_buf[1], wd_buf[:, columns]).astype(BF16).reshape(4, 4, 16, width)
            )
            return carry

        lax.fori_loop(0, 4, chunk, 0)
        send(
            n_refs[flow].at[c, :, :, :, :, pl.ds(0, width)],
            far_refs[flow],
            far_send_sem.at[flow],
            far_recv_sem.at[flow],
            sibling,
        )

    def down_near(flow):
        offset, width, _ = FLOWS[flow]
        arrived(far_refs[flow], far_send_sem.at[flow], far_recv_sem.at[flow])

        def chunk(k, carry):
            columns = pl.ds(pl.multiple_of(k * QUARTER + offset, 128), width)
            total = dot(act_buf[0], wd_buf[:, columns])
            total = total + far_refs[flow][k].reshape(256, width).astype(F32)
            p_refs[flow][k] = total.astype(BF16).reshape(4, 4, 16, width)
            return carry

        lax.fori_loop(0, 4, chunk, 0)
        ring_start(1, flow)

    def add_stream(flow):
        offset, width, _ = FLOWS[flow]
        stream_buf[:, offset : offset + width] += direct_end(1, flow, 2)

    down_far(0)
    for flow in range(6):
        if flow < 5:
            down_far(flow + 1)
        down_near(flow)
        if flow == 4:
            each(ring_pass, 1, FLOW)(0)
    second = (
        each(ring_end, 1, FLOW),
        each(direct_end, 1, FLOW, 1),
        each(add_stream, FLOW),
    )
    each(ring_pass, 1, FLOW)(1)
    for stage in second:
        stage(0)
        stage(1)

    rounded = stream_buf[...].astype(BF16)
    last = jnp.zeros((64, 512), F32)
    for j in range(4):
        pick = onehot(
            (64, 16), lambda i: jnp.where((i % 16) // 4 == j, i // 16 * 4 + i % 4, -1)
        )
        piece = rounded[:, j * 512 : min(j * 512 + 512, QUARTER)]
        moved = dot(pick, piece)
        if moved.shape[1] < 512:
            moved = jnp.concatenate([moved, jnp.zeros((64, 512 - moved.shape[1]), F32)], axis=1)
        last = last + moved
    last_send[...] = last.astype(BF16).reshape(4, 16, 512)
    for step in range(1, 4):
        to = (x + step) % 4
        send(
            last_send.at[to],
            out_ref.at[x],
            last_send_sem.at[step],
            last_recv_sem.at[step],
            device(to, z, y, c),
        )
    out_ref[x] = last_send[x]
    for step in range(1, 4):
        arrived(out_ref.at[(x + 4 - step) % 4], last_send_sem.at[step], last_recv_sem.at[step])
    for copy in sends:
        copy.wait_send()


def per_device(
    queries,
    compressed_cache,
    lengths,
    value_expand_matrix,
    out_proj,
    residual,
    norm_gain,
    expert_ids,
    expert_gates,
    w_gate,
    w_up,
    w_down,
):
    vmem = lambda *shape, dtype=BF16: pltpu.VMEM(shape, dtype)
    widths = [w for _, w, _ in FLOWS]
    dma = lambda *n: pltpu.SemaphoreType.DMA(n)
    scratch = [
        vmem(4, 576, 128),
        vmem(4, 576, 512),
        vmem(256, D),
        vmem(D, 512),
        vmem(D, 512),
        vmem(512, D),
        vmem(4, 512, 256),
        vmem(2, 16, 16, 512),
        vmem(2, 16, 16, 512),
        vmem(1, D, dtype=F32),
        vmem(512, 128, dtype=F32),
        vmem(4, 64, 256),
        vmem(4, 64, 256),
        tuple(vmem(4, 4, 4, 16, w) for w in widths),
        tuple(vmem(2, 2, 4, 16, w) for w in widths),
        tuple(vmem(2, 4, 4, 16, w) for w in widths),
        tuple(vmem(4, 4, 16, w) for w in widths),
        tuple(vmem(3, 4, 16, w) for w in widths),
        tuple(vmem(4, 16, w) for w in widths),
        tuple(vmem(3, 16, w) for w in widths),
        tuple(vmem(2, 4, 4, 4, 16, w + 128 * (f == LAST)) for f, w in enumerate(widths)),
        vmem(16, QUARTER, dtype=F32),
        vmem(2, 256, 512, dtype=F32),
        vmem(2, 256, 512, dtype=F32),
        vmem(2, 256, 512),
        tuple(vmem(4, 4, 4, 16, w) for w in widths),
        vmem(4, 16, 512),
        dma(9),
        dma(4),
        dma(4),
        dma(1),
        dma(1),
        dma(2, 16),
        dma(2, 16),
        dma(4),
        dma(4),
        dma(144),
        dma(144),
        dma(72),
        dma(72),
        dma(6),
        dma(6),
        dma(6),
        dma(6),
        dma(4),
        dma(4),
    ]
    in_vmem = pl.BlockSpec(memory_space=pltpu.VMEM)
    anywhere = pl.BlockSpec(memory_space=pl.ANY)
    result = pl.pallas_call(
        kernel,
        out_shape=jax.ShapeDtypeStruct((4, 16, 512), BF16),
        in_specs=[pl.BlockSpec(memory_space=pltpu.SMEM)] + [in_vmem] * 4 + [anywhere] * 7,
        out_specs=in_vmem,
        scratch_shapes=scratch,
        compiler_params=pltpu.CompilerParams(
            collective_id=0, has_side_effects=True, vmem_limit_bytes=64 << 20
        ),
        cost_estimate=pl.CostEstimate(
            flops=14 * 10**9, bytes_accessed=28 * 10**6, transcendentals=600_000
        ),
        name="layer",
    )(
        lengths,
        residual[0],
        norm_gain,
        expert_ids[0],
        expert_gates[0],
        jnp.swapaxes(queries, 2, 3),
        jnp.swapaxes(compressed_cache, 2, 3),
        value_expand_matrix,
        out_proj,
        w_gate,
        w_up,
        w_down,
    )
    result = result.reshape(4, 4, 4, 512).transpose(2, 0, 1, 3).reshape(4, 4, 2048)
    return result[:, :, :QUARTER].reshape(1, 4, D)


def solution(mesh):
    in_specs = (
        P("grp", "role", None, None),
        P("grp", "role", None, None),
        P("grp", "role"),
        P(("role", "grp"), None, None),
        P(("role", "grp"), None),
        P("grp", "role", None),
        P(),
        P("grp", "role", None),
        P("grp", "role", None),
        P("grp", None, "role"),
        P("grp", None, "role"),
        P("grp", "role", None),
    )
    out_specs = P("grp", "role", None)
    return jax.shard_map(
        per_device, mesh=mesh, in_specs=in_specs, out_specs=out_specs, check_vma=False
    )
```

time: 154 us -> 126 us (0.82)
  Pallas kernels: 140 us -> 125 us
  local copies, waits for them, and re-layouts: 12.2 us -> 1.61 us
    pallas_call x1, Pallas kernels: 140 us -> 125 us  [per_device(): pl.pallas_call(kernel, out_shape=jax.ShapeDtypeStruct((4, 16, 512), BF16)...]
    unnamed x2 -> x0, local copies, waits for them, and re-layouts: 6.48 us -> none
    concatenate x2 -> x0, local copies, waits for them, and re-layouts: 2.76 us -> none  [per_device(): pad = lambda a: jnp.concatenate([a, jnp.zeros_like(a)], axis=0)]
where the time goes in v2:
time: 126 us
  Pallas kernels  125 us (99%)
  local copies, waits for them, and re-layouts  1.61 us (1%)
    pallas_call x1, Pallas kernels, per_device(): pl.pallas_call(kernel, out_shape=jax.ShapeDtypeStruct((4, 16, 512), BF16)...  125 us

profile of v2, /device:TPU:0, one launch (start us, length us, event | category | flops | bytes accessed | tf_op | source)
XLA Modules:
  0.0 126.3 jit_solution(13994071001984683447)
XLA Ops:
  0.0 124.6 %layer.1 = bf16[4,16,512]{2,1,0:T(8,128)(2,1)} custom-call(s32[1,4]{1,0:T(1,128)} %len_ref.1, bf16[4,7168]{1,0:T(4,128)(2,1)} %bitcast.11, bf16[7168]{0:T(1024)(128)(2,1)} %gain_ref.1, s32[4,8]{1,0:T(4,128)} %bitcast.12, bf16[4,8]{1,0:T(4,128)(2,1)} %bitcast.13, bf16[1,4,576,128]{3,2,1,0:T(8,128)(2,1)} %bitcast.10, bf16[1,4,576,512]{3,2,1,0:T(8,128)(2,1)} %bitcast.9, ...), custom_call_target="tpu_custom_call" | custom-call | flops 14000000000 | bytes 28000000 | tf_op jit(solution)/shard_map/layer/pallas_call | solution.py:721
  124.6 0.9 reshape.9
  125.6 0.6 reshape.11
  (3 shorter events, 0.1 us)

commit v3 on v2

--- a/solution.py
+++ b/solution.py
@@ -24,7 +24,18 @@
 )
 LAST = 5
 SETS = ((0, 1, 2), (3, 4, 5))
-LAG = 2
+FIRST_ORDER = tuple((stage, number) for stage in range(6) for number in (0, 1)) + (
+    (6, 0),
+    (7, 0),
+    (6, 1),
+    (8, 0),
+    (9, 0),
+    (7, 1),
+    (10, 0),
+    (8, 1),
+    (9, 1),
+    (10, 1),
+)
 FLOW = object()
 
 
@@ -88,6 +99,7 @@
     act_buf,
     far_refs,
     last_send,
+    last_recv,
     load_sem,
     ve_send_sem,
     ve_recv_sem,
@@ -210,7 +222,7 @@
         a2a_send[pair] = both.astype(BF16)
 
     def a2a_start(pair):
-        def start(step, carry):
+        for step in range(1, 16):
             p, to = zy_peer(step)
             remote(
                 a2a_send.at[pair, p],
@@ -219,13 +231,10 @@
                 a2a_recv_sem.at[pair, step],
                 to,
             ).start()
-            return carry
-
-        lax.fori_loop(1, 16, start, 0)
         a2a_recv[pair, zy] = a2a_send[pair, zy]
 
     def a2a_wait(pair):
-        def wait(step, carry):
+        for step in range(1, 16):
             p, to = zy_peer(16 - step)
             copy = remote(
                 a2a_send.at[pair, zy],
@@ -236,9 +245,6 @@
             )
             copy.wait_send()
             copy.wait_recv()
-            return carry
-
-        lax.fori_loop(1, 16, wait, 0)
 
     attend_pair(0)
     for load in (load_wg, load_wu, load_wd):
@@ -353,12 +359,7 @@
         for k, (step, half) in enumerate(((1, 0), (3, 1))):
             arrived(x_refs[flow].at[k], *rs_sem(round_, flow, k))
             own = p.at[ring_block(flow, ring_at(flow, step), half)]
-
-            def add(i, carry, own=own, k=k):
-                own[i] = (own[i].astype(F32) + x_refs[flow][k, i].astype(F32)).astype(BF16)
-                return carry
-
-            lax.fori_loop(0, 2, add, 0)
+            own[...] = (own[...].astype(F32) + x_refs[flow][k].astype(F32)).astype(BF16)
             send(
                 own,
                 y_refs[flow].at[k, halves[half]],
@@ -373,13 +374,8 @@
             arrived(y_refs[flow].at[k, halves[half]], *rs_sem(round_, flow, 4 + k))
         own = p_refs[flow].at[ring_block(flow, ring_at(flow, 0), None)]
         y_ref = y_refs[flow]
-
-        def add(i, carry):
-            total = own[i].astype(F32) + y_ref[0, i].astype(F32) + y_ref[1, i].astype(F32)
-            s1_refs[flow][i] = total.astype(BF16)
-            return carry
-
-        lax.fori_loop(0, 4, add, 0)
+        total = own[...].astype(F32) + y_ref[0].astype(F32) + y_ref[1].astype(F32)
+        s1_refs[flow][...] = total.astype(BF16)
         direct_start(round_, flow, 1)
 
     def direct_block(flow, phase, index):
@@ -416,14 +412,11 @@
     def project(flow):
         offset, width, _ = FLOWS[flow]
 
-        def chunk(k, carry):
-            columns = pl.ds(pl.multiple_of(k * QUARTER + offset, 128), width)
+        for k in range(4):
+            columns = slice(k * QUARTER + offset, k * QUARTER + offset + width)
             p_refs[flow][k] = dot(rows, op_buf[:, columns]).astype(BF16).reshape(4, 4, 16, width)
             own = p_refs[flow].at[k, z, y]
             own[...] = (own[...].astype(F32) + dot(own_rows, res_ref[:, columns])).astype(BF16)
-            return carry
-
-        lax.fori_loop(0, 4, chunk, 0)
         ring_start(0, flow)
 
     squares = []
@@ -480,12 +473,29 @@
             for k, (step, half) in enumerate(((1, 0), (3, 1), (1, 1), (3, 0))):
                 own = n_refs[flow].at[(c, *ring_block(flow, ring_at(flow, 0), half))]
                 send(own, own, *ag_sem(flow, k), peer(FLOWS[flow][2][0], step))
+            pair_pieces(flow, c, (0,))
+
+    def pair_piece(flow, core, k, index, half):
+        piece = n_refs[flow].at[(core, *ring_block(flow, index, half))]
+        s = flow * 6 + k
+        if core is c:
+            send(piece, piece, pair_send_sem.at[s], pair_recv_sem.at[s], sibling)
+        else:
+            arrived(piece, pair_send_sem.at[s], pair_recv_sem.at[s])
+
+    pieces = ((0, None), (3, 0), (1, 1), (3, 1), (1, 0), (2, None))
+
+    def pair_pieces(flow, core, numbers):
+        for k in numbers:
+            step, half = pieces[k]
+            pair_piece(flow, core, k, ring_at(flow, step), half)
 
     def ag_pass(flow):
         for k, (step, half) in enumerate(((1, 0), (3, 1))):
             got = n_refs[flow].at[(c, *ring_block(flow, ring_at(flow, 4 - step), half))]
             arrived(got, *ag_sem(flow, k))
             send(got, got, *ag_sem(flow, 4 + k), peer(FLOWS[flow][2][0], step))
+        pair_pieces(flow, c, (1, 2))
 
     def ag_last(flow):
         for k, (step, half) in enumerate(((1, 1), (3, 0))):
@@ -494,14 +504,13 @@
         for k, half in enumerate((0, 1)):
             got = n_refs[flow].at[(c, *ring_block(flow, ring_at(flow, 2), half))]
             arrived(got, *ag_sem(flow, 4 + k))
-        half = n_refs[flow].at[c]
-        send(half, half, pair_send_sem.at[flow], pair_recv_sem.at[flow], sibling)
+        pair_pieces(flow, c, (3, 4, 5))
 
     def up(flow, half):
         offset, width, _ = FLOWS[flow]
         core = (c, other)[half]
         if half == 1:
-            arrived(n_refs[flow].at[core], pair_send_sem.at[flow], pair_recv_sem.at[flow])
+            pair_pieces(flow, other, range(6))
         if flow == 0:
             if half == 0:
                 load_wg.wait()
@@ -509,14 +518,12 @@
             acc_g[half] = jnp.zeros((256, 512), F32)
             acc_u[half] = jnp.zeros((256, 512), F32)
 
-        def chunk(k, carry):
-            rows = n_refs[flow][core, k, :, :, :, :width].reshape(256, width)
-            depth = pl.ds(pl.multiple_of(k * QUARTER + offset, 128), width)
-            acc_g[half] += dot(rows, wg_buf[depth, :])
-            acc_u[half] += dot(rows, wu_buf[depth, :])
-            return carry
-
-        lax.fori_loop(0, 4, chunk, 0)
+        rows = jnp.concatenate(
+            [n_refs[flow][core, k, :, :, :, :width].reshape(256, width) for k in range(4)], axis=1
+        )
+        for acc, weights in ((acc_g, wg_buf), (acc_u, wu_buf)):
+            depth = [weights[k * QUARTER + offset : k * QUARTER + offset + width] for k in range(4)]
+            acc[half] += dot(rows, jnp.concatenate(depth, axis=0))
 
     expert = z * 8 + y * 2 + c
     lanes = lax.broadcasted_iota(jnp.int32, (256, 128), 1)
@@ -555,11 +562,8 @@
         each(up, FLOW, 0),
         each(up, FLOW, 1),
     )
-    for tick in range(len(first) + LAG):
-        if tick < len(first):
-            first[tick](0)
-        if tick >= LAG:
-            first[tick - LAG](1)
+    for stage, number in FIRST_ORDER:
+        first[stage](number)
     activate(1)
     activate(0)
 
@@ -572,14 +576,11 @@
     def down_far(flow):
         offset, width, _ = FLOWS[flow]
 
-        def chunk(k, carry):
-            columns = pl.ds(pl.multiple_of(k * QUARTER + offset, 128), width)
+        for k in range(4):
+            columns = slice(k * QUARTER + offset, k * QUARTER + offset + width)
             n_refs[flow][c, k, :, :, :, :width] = (
                 dot(act_buf[1], wd_buf[:, columns]).astype(BF16).reshape(4, 4, 16, width)
             )
-            return carry
-
-        lax.fori_loop(0, 4, chunk, 0)
         send(
             n_refs[flow].at[c, :, :, :, :, pl.ds(0, width)],
             far_refs[flow],
@@ -591,15 +592,11 @@
     def down_near(flow):
         offset, width, _ = FLOWS[flow]
         arrived(far_refs[flow], far_send_sem.at[flow], far_recv_sem.at[flow])
-
-        def chunk(k, carry):
-            columns = pl.ds(pl.multiple_of(k * QUARTER + offset, 128), width)
+        for k in range(4):
+            columns = slice(k * QUARTER + offset, k * QUARTER + offset + width)
             total = dot(act_buf[0], wd_buf[:, columns])
             total = total + far_refs[flow][k].reshape(256, width).astype(F32)
             p_refs[flow][k] = total.astype(BF16).reshape(4, 4, 16, width)
-            return carry
-
-        lax.fori_loop(0, 4, chunk, 0)
         ring_start(1, flow)
 
     def add_stream(flow):
@@ -611,15 +608,11 @@
         if flow < 5:
             down_far(flow + 1)
         down_near(flow)
-        if flow == 4:
-            each(ring_pass, 1, FLOW)(0)
-    second = (
-        each(ring_end, 1, FLOW),
-        each(direct_end, 1, FLOW, 1),
-        each(add_stream, FLOW),
-    )
-    each(ring_pass, 1, FLOW)(1)
-    for stage in second:
+        if flow >= 3:
+            ring_pass(1, flow - 3)
+    for flow in range(3, 6):
+        ring_pass(1, flow)
+    for stage in (each(ring_end, 1, FLOW), each(direct_end, 1, FLOW, 1), each(add_stream, FLOW)):
         stage(0)
         stage(1)
 
@@ -639,14 +632,20 @@
         to = (x + step) % 4
         send(
             last_send.at[to],
-            out_ref.at[x],
+            last_recv.at[x],
             last_send_sem.at[step],
             last_recv_sem.at[step],
             device(to, z, y, c),
         )
-    out_ref[x] = last_send[x]
+    last_recv[x] = last_send[x]
     for step in range(1, 4):
-        arrived(out_ref.at[(x + 4 - step) % 4], last_send_sem.at[step], last_recv_sem.at[step])
+        arrived(last_recv.at[(x + 4 - step) % 4], last_send_sem.at[step], last_recv_sem.at[step])
+    for k in range(4):
+        quarter = last_recv[k].astype(F32)
+        for j in range(4):
+            width = min(512, QUARTER - j * 512)
+            start = k * QUARTER + j * 512
+            out_ref[0, :, start : start + width] = quarter[j * 4 : j * 4 + 4, :width].astype(BF16)
     for copy in sends:
         copy.wait_send()
 
@@ -696,6 +695,7 @@
         vmem(2, 256, 512),
         tuple(vmem(4, 4, 4, 16, w) for w in widths),
         vmem(4, 16, 512),
+        vmem(4, 16, 512),
         dma(9),
         dma(4),
         dma(4),
@@ -709,8 +709,8 @@
         dma(144),
         dma(72),
         dma(72),
-        dma(6),
-        dma(6),
+        dma(36),
+        dma(36),
         dma(6),
         dma(6),
         dma(4),
@@ -720,7 +720,7 @@
     anywhere = pl.BlockSpec(memory_space=pl.ANY)
     result = pl.pallas_call(
         kernel,
-        out_shape=jax.ShapeDtypeStruct((4, 16, 512), BF16),
+        out_shape=jax.ShapeDtypeStruct((1, 4, D), BF16),
         in_specs=[pl.BlockSpec(memory_space=pltpu.SMEM)] + [in_vmem] * 4 + [anywhere] * 7,
         out_specs=in_vmem,
         scratch_shapes=scratch,
@@ -745,8 +745,7 @@
         w_up,
         w_down,
     )
-    result = result.reshape(4, 4, 4, 512).transpose(2, 0, 1, 3).reshape(4, 4, 2048)
-    return result[:, :, :QUARTER].reshape(1, 4, D)
+    return result
 
 
 def solution(mesh):

time: 126 us -> 114 us (0.905)
  Pallas kernels: 125 us -> 112 us
    pallas_call x1, Pallas kernels: 125 us -> 112 us  [per_device(): pl.pallas_call(kernel, out_shape=jax.ShapeDtypeStruct((1, 4, D), BF16), i...]
    reshape x4 -> x0, local copies, waits for them, and re-layouts: 1.59 us -> none  [the longest x3 0.94 us: per_device(): result.reshape(4, 4, 4, 512).transpose(2, 0, 1, 3).reshape(4, 4, 2048)]
    unnamed x0 -> x1, local copies, waits for them, and re-layouts: none -> 1.46 us
where the time goes in v3:
time: 114 us
  Pallas kernels  112 us (98%)
  local copies, waits for them, and re-layouts  1.46 us (1%)
    pallas_call x1, Pallas kernels, per_device(): pl.pallas_call(kernel, out_shape=jax.ShapeDtypeStruct((1, 4, D), BF16), i...  112 us

profile of v3, /device:TPU:0, one launch (start us, length us, event | category | flops | bytes accessed | tf_op | source)
XLA Modules:
  0.0 113.7 jit_solution(11604183873386198892)
XLA Ops:
  0.0 112.3 %layer.1 = bf16[1,4,7168]{2,1,0:T(4,128)(2,1)} custom-call(s32[1,4]{1,0:T(1,128)} %len_ref.1, bf16[4,7168]{1,0:T(4,128)(2,1)} %bitcast.7, bf16[7168]{0:T(1024)(128)(2,1)} %gain_ref.1, s32[4,8]{1,0:T(4,128)} %bitcast.8, bf16[4,8]{1,0:T(4,128)(2,1)} %bitcast.9, bf16[1,4,576,128]{3,2,1,0:T(8,128)(2,1)} %bitcast.6, bf16[1,4,576,512]{3,2,1,0:T(8,128)(2,1)} %bitcast.5, ...), custom_call_target="tpu_custom_call" | custom-call | flops 14000000000 | bytes 28000000 | tf_op jit(solution)/shard_map/layer/pallas_call | solution.py:721
  112.3 1.5 %copy.14 = bf16[1,4,7168]{2,1,0:T(4,128)(2,1)} copy(bf16[1,4,7168]{2,1,0:T(4,128)(2,1)} %layer.1) | data formatting | bytes 114688

commit v4 on v3

--- a/solution.py
+++ b/solution.py
@@ -26,13 +26,13 @@
 SETS = ((0, 1, 2), (3, 4, 5))
 FIRST_ORDER = tuple((stage, number) for stage in range(6) for number in (0, 1)) + (
     (6, 0),
+    (6, 1),
     (7, 0),
-    (6, 1),
+    (7, 1),
     (8, 0),
     (9, 0),
-    (7, 1),
+    (8, 1),
     (10, 0),
-    (8, 1),
     (9, 1),
     (10, 1),
 )
@@ -261,26 +261,24 @@
             ve_recv_sem.at[step],
             device((x + step) % 4, z, y, c),
         )
+    send(ve_own, ve_own, ve_send_sem.at[4], ve_recv_sem.at[4], sibling)
     load_op.wait()
     send(op_own, op_own, op_send_sem.at[0], op_recv_sem.at[0], sibling)
 
     attend_pair(1)
     a2a_start(1)
-    for step in range(1, 4):
-        arrived(
-            ve_buf.at[(x + 4 - step) % 4, :, pl.ds(pl.multiple_of(c * 128, 128), 128)],
-            ve_send_sem.at[step],
-            ve_recv_sem.at[step],
-        )
-    ve_ring = ve_buf.at[:, :, pl.ds(pl.multiple_of(c * 128, 128), 128)]
-    send(ve_ring, ve_ring, ve_send_sem.at[0], ve_recv_sem.at[0], sibling)
+    for step in (1, 3, 2):
+        block = ve_buf.at[(x + 4 - step) % 4, :, pl.ds(pl.multiple_of(c * 128, 128), 128)]
+        arrived(block, ve_send_sem.at[step], ve_recv_sem.at[step])
+        send(block, block, ve_send_sem.at[4 + step], ve_recv_sem.at[4 + step], sibling)
     a2a_wait(0)
     a2a_wait(1)
-    arrived(
-        ve_buf.at[:, :, pl.ds(pl.multiple_of(other * 128, 128), 128)],
-        ve_send_sem.at[0],
-        ve_recv_sem.at[0],
-    )
+    for step in (0, 1, 3, 2):
+        arrived(
+            ve_buf.at[(x + 4 - step) % 4, :, pl.ds(pl.multiple_of(other * 128, 128), 128)],
+            ve_send_sem.at[4 + step],
+            ve_recv_sem.at[4 + step],
+        )
 
     latents = a2a_recv[...].reshape(512, 512)
     head_of_row = lax.broadcasted_iota(jnp.int32, (512, 128), 0) % 8
@@ -532,7 +530,7 @@
         core = (c, other)[half]
         extra = jnp.zeros((256, 128), F32)
         for k in range(4):
-            extra = extra + n_refs[LAST][core, k, :, :, :, 256:].reshape(256, 128).astype(F32)
+            extra = extra + n_refs[LAST][core, k, :, :, :, FLOWS[LAST][1] :].reshape(256, 128).astype(F32)
         weight = jnp.sum(jnp.where(lanes == expert, extra, 0.0), axis=-1, keepdims=True)
         square = jnp.sum(
             jnp.where((lanes == 32) | (lanes == 33), extra, 0.0), axis=-1, keepdims=True
@@ -603,14 +601,13 @@
         offset, width, _ = FLOWS[flow]
         stream_buf[:, offset : offset + width] += direct_end(1, flow, 2)
 
+    count = len(FLOWS)
     down_far(0)
-    for flow in range(6):
-        if flow < 5:
+    for flow in range(count):
+        if flow < count - 1:
             down_far(flow + 1)
         down_near(flow)
-        if flow >= 3:
-            ring_pass(1, flow - 3)
-    for flow in range(3, 6):
+    for flow in range(count):
         ring_pass(1, flow)
     for stage in (each(ring_end, 1, FLOW), each(direct_end, 1, FLOW, 1), each(add_stream, FLOW)):
         stage(0)
@@ -697,8 +694,8 @@
         vmem(4, 16, 512),
         vmem(4, 16, 512),
         dma(9),
-        dma(4),
-        dma(4),
+        dma(8),
+        dma(8),
         dma(1),
         dma(1),
         dma(2, 16),

time: 114 us -> 113 us (level)
  no operation moved by 1% of the time
where the time goes in v4:
time: 113 us
  Pallas kernels  111 us (98%)
  local copies, waits for them, and re-layouts  1.46 us (1%)
    pallas_call x1, Pallas kernels, per_device(): pl.pallas_call(kernel, out_shape=jax.ShapeDtypeStruct((1, 4, D), BF16), i...  111 us

profile of v4, /device:TPU:0, one launch (start us, length us, event | category | flops | bytes accessed | tf_op | source)
XLA Modules:
  0.0 112.9 jit_solution(14224236021986872399)
XLA Ops:
  0.0 111.4 %layer.1 = bf16[1,4,7168]{2,1,0:T(4,128)(2,1)} custom-call(s32[1,4]{1,0:T(1,128)} %len_ref.1, bf16[4,7168]{1,0:T(4,128)(2,1)} %bitcast.7, bf16[7168]{0:T(1024)(128)(2,1)} %gain_ref.1, s32[4,8]{1,0:T(4,128)} %bitcast.8, bf16[4,8]{1,0:T(4,128)(2,1)} %bitcast.9, bf16[1,4,576,128]{3,2,1,0:T(8,128)(2,1)} %bitcast.6, bf16[1,4,576,512]{3,2,1,0:T(8,128)(2,1)} %bitcast.5, ...), custom_call_target="tpu_custom_call" | custom-call | flops 14000000000 | bytes 28000000 | tf_op jit(solution)/shard_map/layer/pallas_call | solution.py:718
  111.4 1.5 %copy.14 = bf16[1,4,7168]{2,1,0:T(4,128)(2,1)} copy(bf16[1,4,7168]{2,1,0:T(4,128)(2,1)} %layer.1) | data formatting | bytes 114688
